TPU v7x, 32 devices: a whole 2x2x4 slice. The times are simulated.
32 devices in a mesh: groups: 2 (over y), fsdp: 4 (over z), tensor: 4 (over x, core).
Axes of the slice: x: 2, y: 2, z: 4, core: 2. Of those that a mesh axis runs over, the one named last changes fastest.
Arguments:
- layer_input_rows: bfloat16 [4, 16, 8192], P(None, ('groups', 'fsdp')), parts along dimension 1, may hold values from -6 to 6
- prenorm_scale: bfloat16 [8192], replicated, may hold values from 0.5 to 1.5
- query_key_value_weight: bfloat16 [8192, 8, 1280], P('fsdp', 'tensor'), may hold values from -0.0625 to 0.0625
- output_weight: bfloat16 [8, 1024, 8192], P('tensor', None, 'fsdp'), may hold values from -0.0625 to 0.0625
- query_down_factor: bfloat16 [64, 8192], P('fsdp'), may hold values from -0.0625 to 0.0625
- query_up_factor: bfloat16 [8, 64, 1024], P('tensor', 'fsdp'), may hold values from -0.29882812 to 0.29882812
- output_down_factor: bfloat16 [8, 64, 1024], P('tensor', 'fsdp'), may hold values from -0.0625 to 0.0625
- output_up_factor: bfloat16 [64, 8192], P('fsdp'), may hold values from -0.29882812 to 0.29882812
- stored_keys: bfloat16 [16, 8, 2048, 128], P(('groups', 'fsdp'), 'tensor'), parts along dimension 0, may hold values from -68 to 68
- stored_values: bfloat16 [16, 8, 2048, 128], P(('groups', 'fsdp'), 'tensor'), parts along dimension 0, may hold values from -6 to 6
- lengths: int32 [16], P(('groups', 'fsdp')), parts along dimension 0, may hold values from 1 to 2048, as said below
Outputs:
- hidden_out: bfloat16 [4, 16, 8192], P(None, ('groups', 'fsdp')), parts along dimension 1
There are 2 independent parts, one for each index of `groups`. A program takes and returns all parts, laid end to end along the dimension named above; an argument that names none is the same for every part. Nothing has to cross between parts.
Inputs may be any that keep to these rules, and one draw needn't show every extreme that they name: `lengths`: some row has exactly 2048 live positions in every draw.
All inputs are finite; a program needn't handle non-finite values.
Results may differ from a plain program's by a relative error of at most 0.013.
The roundings to bfloat16 on the way count: a program that leaves them out, or rounds other values in their place, can miss the bound.
Values may be sent and summed in bfloat16 or wider, within the bound.
No kernel may reach another device: no remote copies, remote signals or barrier semaphores. Data moves between devices by JAX's collectives and lax.ppermute only.
A program may use at most 128 MiB of HBM per device.

v0:
```python
import jax
import jax.numpy as jnp
from jax import lax
from jax.sharding import PartitionSpec as P

QUERY_HEADS = 64
KEY_VALUE_HEADS = 8
HEAD_SIZE = 128


EPS = 1e-05
ADAPTER_SCALE = 2.0


def per_device(
    layer_input_rows,
    prenorm_scale,
    query_key_value_weight,
    output_weight,
    query_down_factor,
    query_up_factor,
    output_down_factor,
    output_up_factor,
    stored_keys,
    stored_values,
    lengths,
):
    q_per_kv = QUERY_HEADS // KEY_VALUE_HEADS
    query_width = q_per_kv * HEAD_SIZE
    span = query_key_value_weight.shape[0]
    local_kv = query_key_value_weight.shape[1]
    step_count = layer_input_rows.shape[0]
    local_rows = layer_input_rows.shape[1]
    full_qa, full_ob = (
        lax.all_gather(query_down_factor, "fsdp", axis=0, tiled=True),
        lax.all_gather(output_up_factor, "fsdp", axis=0, tiled=True),
    )
    offset = lax.axis_index("fsdp") * span
    qa_cols = lax.dynamic_slice_in_dim(full_qa, offset, span, 1)
    ob_cols = lax.dynamic_slice_in_dim(full_ob, offset, span, 1)
    qb_all, oa_all = (
        lax.all_gather(query_up_factor, "fsdp", axis=1, tiled=True),
        lax.all_gather(output_down_factor, "fsdp", axis=1, tiled=True),
    )
    query_update = jnp.einsum("xu,gxw->ugw", qa_cols, qb_all, preferred_element_type=jnp.float32)
    combined_query_weight = (
        query_key_value_weight[:, :, :query_width].astype(jnp.float32)
        + ADAPTER_SCALE * query_update
    ).astype(jnp.bfloat16)
    merged_qkv = jnp.concatenate(
        [combined_query_weight, query_key_value_weight[:, :, query_width:]], axis=2
    )
    flat_qkv = merged_qkv.reshape(span, local_kv * (q_per_kv + 2) * HEAD_SIZE)
    output_update = jnp.einsum("xts,tz->xsz", oa_all, ob_cols, preferred_element_type=jnp.float32)
    combined_output_weight = (
        output_weight.astype(jnp.float32) + ADAPTER_SCALE * output_update
    ).astype(jnp.bfloat16)
    flat_out = combined_output_weight.reshape(local_kv * query_width, span)
    positions = jnp.arange(stored_keys.shape[2], dtype=jnp.int32)
    valid = positions[None, :] < lengths[:, None]
    score_scale = 1.0 / HEAD_SIZE**0.5
    tok_rows = jnp.transpose(layer_input_rows, (1, 0, 2)).astype(jnp.float32)
    spread_sq = jnp.mean(tok_rows * tok_rows, axis=-1, keepdims=True)
    normed = (tok_rows * lax.rsqrt(spread_sq + EPS) * prenorm_scale.astype(jnp.float32)).astype(
        jnp.bfloat16
    )
    spread_rows = lax.all_to_all(normed, "fsdp", split_axis=2, concat_axis=0, tiled=True)
    flat = spread_rows.reshape(local_rows * lax.axis_size("fsdp") * step_count, span)
    projected = lax.psum_scatter(
        jnp.dot(flat, flat_qkv, preferred_element_type=jnp.float32).reshape(
            local_rows * lax.axis_size("fsdp"), step_count, -1
        ),
        "fsdp",
        scatter_dimension=0,
        tiled=True,
    ).astype(jnp.bfloat16)
    projected = projected.reshape(local_rows, step_count, local_kv, q_per_kv + 2, HEAD_SIZE)
    query = projected[:, :, :, :q_per_kv]
    win_keys = projected[:, :, :, q_per_kv]
    win_values = projected[:, :, :, q_per_kv + 1]
    score_cache = (
        jnp.einsum("rskgh,rklh->rskgl", query, stored_keys, preferred_element_type=jnp.float32)
        * score_scale
    )
    score_cache = jnp.where(valid[:, None, None, None, :], score_cache, -1e30)
    score_win = (
        jnp.einsum("rskgh,rtkh->rskgt", query, win_keys, preferred_element_type=jnp.float32)
        * score_scale
    )
    step_ids = jnp.arange(step_count, dtype=jnp.int32)
    causal = step_ids[None, :] <= step_ids[:, None]
    score_win = jnp.where(causal[None, :, None, None, :], score_win, -1e30)
    peak = jnp.maximum(jnp.max(score_cache, axis=-1), jnp.max(score_win, axis=-1))
    exp_cache = jnp.exp(score_cache - peak[..., None])
    exp_win = jnp.exp(score_win - peak[..., None])
    total = jnp.sum(exp_cache, axis=-1) + jnp.sum(exp_win, axis=-1)
    weight_cache = (exp_cache / total[..., None]).astype(jnp.bfloat16)
    weight_win = (exp_win / total[..., None]).astype(jnp.bfloat16)
    context = jnp.einsum(
        "rskgl,rklh->rskgh", weight_cache, stored_values, preferred_element_type=jnp.float32
    )
    context = context + jnp.einsum(
        "rskgt,rtkh->rskgh", weight_win, win_values, preferred_element_type=jnp.float32
    )
    context = context.astype(jnp.bfloat16).reshape(local_rows, step_count, local_kv * query_width)
    piece = lax.all_gather(context, "fsdp", axis=0, tiled=True)
    flat = piece.reshape(piece.shape[0] * step_count, local_kv * query_width)
    partial_out = jnp.dot(flat, flat_out, preferred_element_type=jnp.float32).reshape(
        piece.shape[0], step_count, span
    )
    summed = lax.psum(partial_out.astype(jnp.bfloat16), "tensor").astype(jnp.float32)
    attended = lax.all_to_all(summed, "fsdp", split_axis=0, concat_axis=2, tiled=True)
    result = (tok_rows + attended).astype(jnp.bfloat16)
    return jnp.transpose(result, (1, 0, 2))


def solution(mesh):
    placed = (
        P(None, ("groups", "fsdp"), None),
        P(),
        P("fsdp", "tensor", None),
        P("tensor", None, "fsdp"),
        P("fsdp", None),
        P("tensor", "fsdp", None),
        P("tensor", "fsdp", None),
        P("fsdp", None),
        P(("groups", "fsdp"), "tensor", None, None),
        P(("groups", "fsdp"), "tensor", None, None),
        P(("groups", "fsdp")),
    )
    return jax.shard_map(
        per_device,
        mesh=mesh,
        in_specs=placed,
        out_specs=P(None, ("groups", "fsdp"), None),
        check_vma=False,
    )
```

profile of v0, /device:TPU:0, one launch (start us, length us, event | category | flops | bytes accessed | tf_op | source)
XLA Modules:
  0.0 301.3 jit_solution(15276049586085288954)
XLA Ops:
  7.3 8.7 %copy.43 = f32[4,2,8192]{0,1,2:T(2,128)} copy(bf16[4,2,8192]{2,1,0:T(2,128)(2,1)} %param.11) | data formatting | bytes 393216 | tf_op jit(solution)/shard_map/convert_element_type | solution.py:62
  16.0 11.3 %fusion.2 = f32[2,4]{1,0:T(2,128)S(1)} fusion(f32[4,2,8192]{0,1,2:T(2,128)} %copy.43), kind=kLoop, calls=%fused_computation.8 | loop fusion | flops 131064 | bytes 262176 | tf_op jit(solution)/shard_map/reduce_sum | solution.py:63
  27.4 24.5 %fusion.35 = bf16[8192,2,4]{2,1,0:T(2,128)(2,1)} fusion(f32[8192]{0:T(1024)S(1)} %convert_element_type.47, f32[2,4]{1,0:T(2,128)S(1)} %add_rsqrt_fusion, f32[4,2,8192]{0,1,2:T(2,128)S(1)} %copy-done.1), kind=kLoop, calls=%fused_computation.53 | loop fusion | flops 196608 | bytes 426016
  51.9 9.3 %reshape.82 = bf16[4,2,8192]{2,1,0:T(2,128)(2,1)} reshape(bf16[8192,2,4]{2,1,0:T(2,128)(2,1)} %fusion.35) | data formatting | bytes 262144
  61.2 6.2 %all-to-all-start = ((bf16[4,2,8192]{2,1,0:T(2,128)(2,1)}), bf16[4,2,8192]{2,1,0:T(2,128)(2,1)S(1)}, u32[]{:S(2)}, u32[]{:S(2)}) async-start(bf16[4,2,8192]{2,1,0:T(2,128)(2,1)} %reshape.82), calls=%async_computation | async-start | bytes 262144 | tf_op jit(solution)/shard_map/all_to_all | solution.py:67
  68.2 8.0 %slice.15 = bf16[2048,2,1024]{2,1,0:T(2,128)(2,1)} slice(bf16[2048,2,1280]{2,1,0:T(2,128)(2,1)} %param.13), slice={[0:2048], [0:2], [0:1024]} | slice | bytes 16777216 | tf_op jit(solution)/shard_map/slice | solution.py:47
  76.2 4.5 %slice.16 = bf16[2048,2,256]{2,1,0:T(2,128)(2,1)} slice(bf16[2048,2,1280]{2,1,0:T(2,128)(2,1)} %param.13), slice={[0:2048], [0:2], [1024:1280]} | slice | bytes 4194304 | tf_op jit(solution)/shard_map/slice | solution.py:51
  80.7 21.3 %copy.67 = bf16[2048,2,1024]{0,2,1:T(8,128)(2,1)} copy(bf16[2048,2,1024]{2,1,0:T(2,128)(2,1)} %slice.15) | data formatting | bytes 16777216
  102.0 14.5 %all_gather.16 = bf16[2,64,1024]{2,1,0:T(8,128)(2,1)S(1)} all-gather(bf16[2,16,1024]{2,1,0:T(8,128)(2,1)S(1)} %copy-done.3), channel_id=1, replica_groups=mesh['groups'=2,'fsdp'=4,'tensor'=4] {'fsdp'}, dimensions={1}, use_global_device_ids=true | all-gather | bytes 327680 | tf_op jit(solution)/shard_map/all_gather | solution.py:42
  116.5 6.2 %copy.68 = bf16[2048,2,256]{0,2,1:T(8,128)(2,1)} copy(bf16[2048,2,256]{2,1,0:T(2,128)(2,1)} %slice.16) | data formatting | bytes 4194304
  124.0 14.3 %all_gather.19 = bf16[2,64,1024]{2,1,0:T(8,128)(2,1)S(1)} all-gather(bf16[2,16,1024]{2,1,0:T(8,128)(2,1)S(1)} %copy-done.4), channel_id=1, replica_groups=mesh['groups'=2,'fsdp'=4,'tensor'=4] {'fsdp'}, dimensions={1}, use_global_device_ids=true | all-gather | bytes 327680 | tf_op jit(solution)/shard_map/all_gather | solution.py:43
  138.4 10.0 %reshape.83 = bf16[8192,2,4]{2,1,0:T(2,128)(2,1)} reshape(bf16[4,2,8192]{2,1,0:T(2,128)(2,1)S(1)} %all-to-all-done) | data formatting | bytes 262144
  148.4 9.7 %copy.64 = bf16[4,2,4,2048]{3,2,1,0:T(4,128)(2,1)S(1)} copy(bf16[4,2,4,2048]{2,1,3,0:T(2,128)(2,1)} %bitcast.97) | data formatting | bytes 262144 | tf_op jit(solution)/shard_map/dot_general | solution.py:70
  158.1 5.0 %add_convert_fusion = bf16[2048,2,1024]{0,2,1:T(8,128)(2,1)S(1)} fusion(bf16[2048,2,1024]{0,2,1:T(8,128)(2,1)} %copy.67, bf16[2,64,1024]{2,1,0:T(8,128)(2,1)S(1)} %all_gather.16, bf16[64,8192]{1,0:T(8,128)(2,1)} %all-gather.3.cloned.1.call-done, s32[]{:T(128)S(6)} %select_n.15), kind=kOutput, calls=%fused_computation.2 | convolution fusion | flops 553648128 | bytes 17301508 | tf_op jit(solution)/shard_map/xu,gxw->ugw/dot_general | solution.py:45
  163.1 8.0 %pad_maximum_fusion = bf16[2048,2,1280]{0,2,1:T(8,128)(2,1)S(1)} fusion(bf16[2048,2,256]{0,2,1:T(8,128)(2,1)S(1)} %copy-done.2, bf16[2048,2,1024]{0,2,1:T(8,128)(2,1)S(1)} %add_convert_fusion), kind=kLoop, calls=%fused_computation.3 | loop fusion | flops 20971520 | bytes 20971520 | tf_op jit(solution)/shard_map/concatenate | solution.py:50
  171.2 3.3 %fusion.36 = f32[8,4,2560]{2,1,0:T(4,128)S(1)} fusion(bf16[8,4,2048]{2,1,0:T(4,128)(2,1)S(1)} %bitcast.99, bf16[2048,2560,1]{0,1,2:T(8,128)(2,1)S(1)} %bitcast.94), kind=kOutput, calls=%fused_computation.54 | convolution fusion | flops 335544320 | bytes 10944512 | tf_op jit(solution)/shard_map/dot_general | solution.py:70
  174.5 26.1 %all-reduce.5 = bf16[8,4,2560]{2,1,0:T(4,128)(2,1)S(1)} all-reduce(f32[8,4,2560]{2,1,0:T(4,128)S(1)} %fusion.36), channel_id=2, replica_groups=mesh['groups'=2,'fsdp'=4,'tensor'=4] {'fsdp'}, use_global_device_ids=true, to_apply=%region_1.0.clone | all-reduce | flops 81920 | bytes 491520
  204.6 13.4 %all_gather.17 = bf16[8,4,2048]{2,1,0:T(4,128)(2,1)S(1)} all-gather(bf16[2,4,2048]{2,1,0:T(4,128)(2,1)S(1)} %reshape.71), channel_id=1, replica_groups=mesh['groups'=2,'fsdp'=4,'tensor'=4] {'fsdp'}, dimensions={0}, use_global_device_ids=true | all-gather | bytes 163840 | tf_op jit(solution)/shard_map/all_gather | solution.py:106
  218.0 4.9 %fusion = bf16[2,1024,2048]{2,1,0:T(8,128)(2,1)S(1)} fusion(bf16[2,1024,2048]{2,1,0:T(8,128)(2,1)} %param.14, bf16[2,64,1024]{2,1,0:T(8,128)(2,1)S(1)} %all_gather.19, bf16[64,8192]{1,0:T(8,128)(2,1)} %all-gather.5.cloned.1.call-done, s32[]{:T(128)S(6)} %select_n.15), kind=kOutput, calls=%fused_computation.1 | convolution fusion | flops 553648128 | bytes 17301508 | tf_op jit(solution)/shard_map/xts,tz->xsz/dot_general | solution.py:54
  225.0 29.8 %all-reduce.4.cloned.1.call-done = bf16[8,4,2048]{2,0,1:T(8,128)(2,1)} async-done(((bf16[8,4,2048]{2,0,1:T(8,128)(2,1)}), bf16[8,4,2048]{2,0,1:T(8,128)(2,1)}) %all-reduce.4.cloned.1.call-update) | async-done | bytes 131088 | tf_op jit(solution)/shard_map/psum | solution.py:111
  255.8 12.2 %all_to_all.33 = f32[8,4,2048]{2,1,0:T(4,128)S(1)} all-to-all(f32[8,4,2048]{2,1,0:T(4,128)S(1)} %copy.54), channel_id=1, replica_groups=mesh['groups'=2,'fsdp'=4,'tensor'=4] {'fsdp'}, dimensions={0} | all-to-all | bytes 524288 | tf_op jit(solution)/shard_map/all_to_all | solution.py:112
  268.0 8.6 %copy.55 = f32[4,2,4,2048]{2,1,3,0:T(2,128)} copy(f32[4,2,4,2048]{3,2,1,0:T(4,128)S(1)} %bitcast.98) | data formatting | bytes 524288 | tf_op jit(solution)/shard_map/all_to_all | solution.py:112
  276.6 8.9 %fusion.1 = bf16[2,4,8192]{1,0,2:T(2,128)(2,1)} fusion(f32[4,2,4,2048]{2,1,3,0:T(2,128)} %copy.55, f32[4,2,8192]{0,1,2:T(2,128)} %copy.43), kind=kLoop, calls=%fused_computation.5 | loop fusion | flops 131072 | bytes 655360 | tf_op jit(solution)/shard_map/convert_element_type | solution.py:113
  285.5 9.3 %copy.56 = bf16[4,2,8192]{2,1,0:T(2,128)(2,1)} copy(bf16[4,2,8192]{0,1,2:T(2,128)(2,1)} %bitcast.96) | data formatting | bytes 262144 | tf_op jit(solution)/shard_map/transpose | solution.py:114
  (45 shorter events, 9.3 us)
Async XLA Ops:
  6.5 194.5 %copy-start = (bf16[2,2,2048,128]{3,2,1,0:T(8,128)(2,1)S(1)}, bf16[2,2,2048,128]{3,2,1,0:T(8,128)(2,1)}, u32[]{:S(2)}) copy-start(bf16[2,2,2048,128]{3,2,1,0:T(8,128)(2,1)} %param.19) | copy-start | bytes 6291460
  6.5 151.6 %all-gather.3.cloned.1.call-start = ((), (), s32[]{:S(2)}) async-start(), calls=%async_computation.2 | async-start | bytes 1310720 | tf_op jit(solution)/shard_map/all_gather | solution.py:35
  7.3 20.1 %copy-start.5 = (bf16[8192]{0:T(1024)(128)(2,1)S(1)}, bf16[8192]{0:T(1024)(128)(2,1)}, u32[]{:S(2)}) copy-start(bf16[8192]{0:T(1024)(128)(2,1)} %param.12) | copy-start | bytes 49156
  16.0 11.4 %copy-start.1 = (f32[4,2,8192]{0,1,2:T(2,128)S(1)}, f32[4,2,8192]{0,1,2:T(2,128)}, u32[]{:S(2)}) copy-start(f32[4,2,8192]{0,1,2:T(2,128)} %copy.43) | copy-start | bytes 786436
  61.2 77.2 %all-to-all-start = ((bf16[4,2,8192]{2,1,0:T(2,128)(2,1)}), bf16[4,2,8192]{2,1,0:T(2,128)(2,1)S(1)}, u32[]{:S(2)}, u32[]{:S(2)}) async-start(bf16[4,2,8192]{2,1,0:T(2,128)(2,1)} %reshape.82), calls=%async_computation | async-start | bytes 262144 | tf_op jit(solution)/shard_map/all_to_all | solution.py:67
  67.4 150.6 %all-gather.5.cloned.1.call-start = ((), (), s32[]{:S(2)}) async-start(), calls=%async_computation.3 | async-start | bytes 1310720 | tf_op jit(solution)/shard_map/all_gather | solution.py:36
  68.2 186.6 %all-reduce.4.cloned.1.call-start = ((), (), s32[]{:S(2)}) async-start(), calls=%async_computation.4 | async-start | bytes 262144 | tf_op jit(solution)/shard_map/psum | solution.py:111
  80.7 21.3 %copy-start.3 = (bf16[2,16,1024]{2,1,0:T(8,128)(2,1)S(1)}, bf16[2,16,1024]{2,1,0:T(8,128)(2,1)}, u32[]{:S(2)}) copy-start(bf16[2,16,1024]{2,1,0:T(8,128)(2,1)} %param.16) | copy-start | bytes 196612
  80.7 42.0 %copy-start.6 = (s32[2]{0:T(128)S(1)}, s32[2]{0:T(128)}, u32[]{:S(2)}) copy-start(s32[2]{0:T(128)} %param.21) | copy-start | bytes 28
  80.7 42.1 %copy-start.7 = (u32[32]{0:T(128)S(1)}, u32[32]{0:T(128)}, u32[]{:S(2)}) copy-start(u32[32]{0:T(128)} %constant.38) | copy-start | bytes 388
  80.7 43.3 %copy-start.4 = (bf16[2,16,1024]{2,1,0:T(8,128)(2,1)S(1)}, bf16[2,16,1024]{2,1,0:T(8,128)(2,1)}, u32[]{:S(2)}) copy-start(bf16[2,16,1024]{2,1,0:T(8,128)(2,1)} %param.17) | copy-start | bytes 196612
  158.1 5.0 %copy-start.2 = (bf16[2048,2,256]{0,2,1:T(8,128)(2,1)S(1)}, bf16[2048,2,256]{0,2,1:T(8,128)(2,1)}, u32[]{:S(2)}) copy-start(bf16[2048,2,256]{0,2,1:T(8,128)(2,1)} %copy.68) | copy-start | bytes 6291460
Sparse Core Ops, SparseCore 0:
  8.9 30.6 all-gather.2
  69.8 29.3 all-gather.4
  225.1 29.6 all-reduce.3
where the time goes:
time: 303 us; the launch traced here: 301 us
  local copies, waits for them, and re-layouts  97.3 us (32%)
  blocking collectives  80.6 us (27%)
  other arithmetic  53.2 us (18%)
  waiting for transfers between devices  31.3 us (10%)
  matrix products  18.8 us (6%)
  between operations  13.9 us (5%)
  starting transfers between devices  6.27 us (2%)
    unnamed x21, local copies, waits for them, and re-layouts  47.4 us
    psum x1, waiting for transfers between devices, per_device(): lax.psum(partial_out.astype(jnp.bfloat16), 'tensor').astype(jnp.float32)  29.8 us
    unnamed x1, blocking collectives  26.1 us
    unnamed x1, other arithmetic  24.5 us
    all_gather x1, blocking collectives, per_device(): lax.all_gather(query_up_factor, 'fsdp', axis=1, tiled=True)  14.5 us
    all_gather x1, blocking collectives, per_device(): lax.all_gather(output_down_factor, 'fsdp', axis=1, tiled=True)  14.3 us
    all_gather x1, blocking collectives, per_device(): piece = lax.all_gather(context, 'fsdp', axis=0, tiled=True)  13.4 us
    all_to_all x1, blocking collectives, per_device(): lax.all_to_all(summed, 'fsdp', split_axis=0, concat_axis=2, tiled=True)  12.2 us
  transfers between devices with their start and end apart: 4, of which 1 were waited for; matrix products, arithmetic and copies ran while one was open for 45% of the time, Pallas kernels for 0%

commit v1 on v0

v1 whole, which is shorter than its diff:
```python
import functools

import jax
import jax.numpy as jnp
from jax import lax
from jax.experimental import pallas as pl
from jax.experimental.pallas import tpu as pltpu
from jax.sharding import PartitionSpec as P

QUERY_HEADS = 64
KEY_VALUE_HEADS = 8
HEAD_SIZE = 128
EPS = 1e-05
ADAPTER_SCALE = 2.0

GROUP = QUERY_HEADS // KEY_VALUE_HEADS
QUERY_WIDTH = GROUP * HEAD_SIZE
HEAD_WIDTH = QUERY_WIDTH + 2 * HEAD_SIZE
F32 = jnp.float32
BF16 = jnp.bfloat16
MIB = 2**20
VMEM = pl.BlockSpec(memory_space=pltpu.VMEM)
SMEM = pl.BlockSpec(memory_space=pltpu.SMEM)
ANY = pl.BlockSpec(memory_space=pl.ANY)


def params(mib):
    return pltpu.CompilerParams(vmem_limit_bytes=mib * MIB)


def dot(a, b):
    return jnp.dot(a, b, preferred_element_type=F32)


def dot_nt(a, b):
    return lax.dot_general(a, b, (((1,), (1,)), ((), ())), preferred_element_type=F32)


def dot_split(a, b):
    high = a.astype(BF16)
    low = (a - high.astype(F32)).astype(BF16)
    return dot(high, b) + dot(low, b)


def swap(x, axis, mask):
    size = lax.axis_size(axis)
    return lax.ppermute(x, axis, [(i, i ^ mask) for i in range(size)])


def pack_kernel(ranks, parts, index, down, up, *outs):
    heads = down.shape[0]
    width = outs[0].shape[1] - heads * QUERY_WIDTH
    for j in range(parts):
        for k in range(heads):
            outs[j][:, k * QUERY_WIDTH : (k + 1) * QUERY_WIDTH] = down[k]
        start = pl.multiple_of((index[0] ^ j) * width, 128)
        outs[j][:, heads * QUERY_WIDTH :] = up[:, pl.ds(start, width)]


def project_kernel(parts, blocks, index, *refs):
    x = refs[:parts]
    scale, weight, down, up = refs[parts : parts + 4]
    outs = refs[parts + 4 : 2 * parts + 4]
    normed, wide, buf, sems = refs[2 * parts + 4 :]
    span, heads = weight.shape[:2]
    steps, rows, width = x[0].shape
    tokens = steps * rows
    total = parts * tokens
    chunk = span // blocks
    copies = [
        pltpu.make_async_copy(
            weight.at[pl.ds(b * chunk, chunk)], buf.at[pl.ds(b * chunk, chunk)], sems.at[b]
        )
        for b in range(blocks)
    ]
    for copy in copies:
        copy.start()

    gain = scale[...].astype(F32).reshape(1, width)
    for j in range(0, parts, 2):
        pair = []
        for i in (j, j + 1):
            values = x[i][...].astype(F32).reshape(tokens, width)
            spread = jnp.mean(values * values, axis=-1, keepdims=True)
            pair.append(values * lax.rsqrt(spread + EPS) * gain)
        normed[j * tokens : (j + 2) * tokens, :] = jnp.concatenate(pair, axis=0).astype(BF16)

    low_rank = dot_nt(normed[...], down[...])

    start = pl.multiple_of(index[0] * span, 128)
    mine = normed[:, pl.ds(start, span)]
    pieces = span // HEAD_SIZE
    if heads == 1:
        wide[...] = mine
    else:
        stacked = jnp.concatenate(
            [mine[:, c * HEAD_SIZE : (c + 1) * HEAD_SIZE] for c in range(pieces)], axis=0
        )
        spot = lax.broadcasted_iota(jnp.int32, (HEAD_SIZE, heads * HEAD_SIZE), 1)
        line = lax.broadcasted_iota(jnp.int32, (HEAD_SIZE, heads * HEAD_SIZE), 0)
        for k in range(heads):
            place = jnp.where(spot == line * heads + k, 1.0, 0.0).astype(BF16)
            spread_out = dot(stacked, place).astype(BF16)
            for c in range(pieces):
                wide[
                    k * total : (k + 1) * total,
                    c * heads * HEAD_SIZE : (c + 1) * heads * HEAD_SIZE,
                ] = spread_out[c * total : (c + 1) * total]

    sums = None
    for b in range(blocks):
        copies[b].wait()
        tile = buf[pl.ds(b * chunk, chunk)].reshape(chunk * heads, HEAD_WIDTH)
        part = dot(wide[:, b * chunk * heads : (b + 1) * chunk * heads], tile)
        sums = part if b == 0 else sums + part
    for k in range(heads):
        update = ADAPTER_SCALE * dot_split(low_rank, up[k])
        for j in range(parts):
            here = sums[k * total + j * tokens : k * total + (j + 1) * tokens]
            outs[j][:, k * HEAD_WIDTH : k * HEAD_WIDTH + QUERY_WIDTH] = (
                here[:, :QUERY_WIDTH] + update[j * tokens : (j + 1) * tokens]
            )
            outs[j][:, k * HEAD_WIDTH + QUERY_WIDTH : (k + 1) * HEAD_WIDTH] = here[:, QUERY_WIDTH:]


def attend_kernel(parts, rows, lengths, *refs):
    sums = refs[:parts]
    keys, values, out = refs[parts : parts + 3]
    heads, cache = keys.shape[1:3]
    tokens = out.shape[0]
    projected = sums[0][...]
    for j in range(1, parts):
        projected = projected + sums[j][...]
    lines = GROUP * tokens
    row_of = lax.broadcasted_iota(jnp.int32, (lines, 1), 0) % rows
    position = lax.broadcasted_iota(jnp.int32, (lines, cache), 1)
    limit = jnp.zeros((lines, 1), jnp.int32)
    for r in range(rows):
        limit = jnp.where(row_of == r, lengths[r], limit)
    live = position < limit
    asks = lax.broadcasted_iota(jnp.int32, (lines, tokens), 0) % tokens
    tells = lax.broadcasted_iota(jnp.int32, (lines, tokens), 1)
    seen = (asks % rows == tells % rows) & (tells // rows <= asks // rows)
    scale = 1.0 / HEAD_SIZE**0.5

    def pick(parts_of):
        result = parts_of[0]
        for r in range(1, rows):
            result = jnp.where(row_of == r, parts_of[r], result)
        return result

    for k in range(heads):
        base = k * HEAD_WIDTH
        query = jnp.concatenate(
            [projected[:, base + g * HEAD_SIZE : base + (g + 1) * HEAD_SIZE] for g in range(GROUP)],
            axis=0,
        ).astype(BF16)
        new_keys = projected[:, base + QUERY_WIDTH : base + QUERY_WIDTH + HEAD_SIZE].astype(BF16)
        new_values = projected[:, base + QUERY_WIDTH + HEAD_SIZE : base + HEAD_WIDTH].astype(BF16)
        scores = pick([dot_nt(query, keys[r, k]) for r in range(rows)]) * scale
        scores = jnp.where(live, scores, -1e30)
        window = jnp.where(seen, dot_nt(query, new_keys) * scale, -1e30)
        peak = jnp.maximum(
            jnp.max(scores, axis=-1, keepdims=True), jnp.max(window, axis=-1, keepdims=True)
        )
        exp_cache = jnp.exp(scores - peak)
        exp_window = jnp.exp(window - peak)
        total = jnp.sum(exp_cache, axis=-1, keepdims=True) + jnp.sum(
            exp_window, axis=-1, keepdims=True
        )
        share = 1.0 / total
        weights = (exp_cache * share).astype(BF16)
        weights_window = (exp_window * share).astype(BF16)
        context = pick([dot(weights, values[r, k]) for r in range(rows)])
        context = context + dot(weights_window, new_values)
        for g in range(GROUP):
            first = k * QUERY_WIDTH + g * HEAD_SIZE
            out[:, first : first + HEAD_SIZE] = context[g * tokens : (g + 1) * tokens].astype(BF16)


def output_kernel(parts, blocks, *refs):
    contexts = refs[:parts]
    factors = refs[parts : 2 * parts]
    weight = refs[2 * parts]
    outs = refs[2 * parts + 1 : 3 * parts + 1]
    buf, sems = refs[3 * parts + 1 :]
    depth, width = weight.shape
    tokens = contexts[0].shape[0]
    chunk = depth // blocks
    copies = [
        pltpu.make_async_copy(
            weight.at[pl.ds(b * chunk, chunk)], buf.at[pl.ds(b * chunk, chunk)], sems.at[b]
        )
        for b in range(blocks)
    ]
    for copy in copies:
        copy.start()
    context = jnp.concatenate([c[...].astype(F32) for c in contexts], axis=0).astype(BF16)
    sums = None
    for j in range(parts):
        inner = dot_nt(context, factors[j][:, :depth])
        part = dot_split(inner, factors[j][:, depth:])
        sums = part if j == 0 else sums + part
    sums = ADAPTER_SCALE * sums
    for b in range(blocks):
        copies[b].wait()
        sums = sums + dot(context[:, b * chunk : (b + 1) * chunk], buf[pl.ds(b * chunk, chunk)])
    for j in range(parts):
        outs[j][...] = sums[j * tokens : (j + 1) * tokens].astype(BF16)


def gather_kernel(parts, *refs):
    out = refs[parts]
    width = refs[0].shape[1]
    for j in range(parts):
        out[:, j * width : (j + 1) * width] = refs[j][...]


def finish_kernel(parts, teams, index, x, *refs):
    pieces = refs[:teams]
    out = refs[teams]
    steps, rows, whole = x.shape
    width = whole // parts
    for j in range(parts):
        start = pl.multiple_of((index[0] ^ j) * width, 128)
        attended = pieces[0][:, j * width : (j + 1) * width].astype(F32)
        for t in range(1, teams):
            attended = attended + pieces[t][:, j * width : (j + 1) * width].astype(F32)
        result = x[:, :, pl.ds(start, width)].astype(F32) + attended.reshape(steps, rows, width)
        out[:, :, pl.ds(start, width)] = result.astype(BF16)


def per_device(
    layer_input_rows,
    prenorm_scale,
    query_key_value_weight,
    output_weight,
    query_down_factor,
    query_up_factor,
    output_down_factor,
    output_up_factor,
    stored_keys,
    stored_values,
    lengths,
):
    parts = lax.axis_size("fsdp")
    teams = lax.axis_size("tensor")
    steps, rows, model = layer_input_rows.shape
    tokens = steps * rows
    span, heads = query_key_value_weight.shape[:2]
    ranks = query_down_factor.shape[0]
    index = lax.axis_index("fsdp").astype(jnp.int32).reshape(1)

    x = [layer_input_rows] + [swap(layer_input_rows, "fsdp", j) for j in range(1, parts)]

    factor_width = heads * QUERY_WIDTH + span
    packs = pl.pallas_call(
        functools.partial(pack_kernel, ranks, parts),
        out_shape=[jax.ShapeDtypeStruct((ranks, factor_width), BF16)] * parts,
        in_specs=[SMEM, VMEM, VMEM],
        out_specs=[VMEM] * parts,
        compiler_params=params(16),
        name="pack_factors",
    )(index, output_down_factor, output_up_factor)
    factors = [packs[0]] + [swap(packs[j], "fsdp", j) for j in range(1, parts)]

    blocks = 8
    sums = pl.pallas_call(
        functools.partial(project_kernel, parts, blocks),
        out_shape=[jax.ShapeDtypeStruct((tokens, heads * HEAD_WIDTH), F32)] * parts,
        in_specs=[SMEM] + [VMEM] * parts + [VMEM, ANY, VMEM, VMEM],
        out_specs=[VMEM] * parts,
        scratch_shapes=[
            pltpu.VMEM((parts * tokens, model), BF16),
            pltpu.VMEM((heads * parts * tokens, heads * span), BF16),
            pltpu.VMEM((span, heads, HEAD_WIDTH), BF16),
            pltpu.SemaphoreType.DMA((blocks,)),
        ],
        compiler_params=params(48),
        name="norm_project",
    )(index, *x, prenorm_scale, query_key_value_weight, query_down_factor, query_up_factor)
    sums = [sums[0]] + [swap(sums[j], "fsdp", j) for j in range(1, parts)]

    context = pl.pallas_call(
        functools.partial(attend_kernel, parts, rows),
        out_shape=jax.ShapeDtypeStruct((tokens, heads * QUERY_WIDTH), BF16),
        in_specs=[SMEM] + [VMEM] * parts + [VMEM, VMEM],
        out_specs=VMEM,
        compiler_params=params(32),
        name="attend",
    )(lengths, *sums, stored_keys, stored_values)
    contexts = [context] + [swap(context, "fsdp", j) for j in range(1, parts)]

    partial = pl.pallas_call(
        functools.partial(output_kernel, parts, blocks),
        out_shape=[jax.ShapeDtypeStruct((tokens, span), BF16)] * parts,
        in_specs=[VMEM] * (2 * parts) + [ANY],
        out_specs=[VMEM] * parts,
        scratch_shapes=[
            pltpu.VMEM((heads * QUERY_WIDTH, span), BF16),
            pltpu.SemaphoreType.DMA((blocks,)),
        ],
        compiler_params=params(48),
        name="project_out",
    )(*contexts, *factors, output_weight.reshape(heads * QUERY_WIDTH, span))
    partial = [partial[0]] + [swap(partial[j], "fsdp", j) for j in range(1, parts)]

    gathered = pl.pallas_call(
        functools.partial(gather_kernel, parts),
        out_shape=jax.ShapeDtypeStruct((tokens, model), BF16),
        in_specs=[VMEM] * parts,
        out_specs=VMEM,
        compiler_params=params(16),
        name="gather_columns",
    )(*partial)
    pieces = [gathered] + [swap(gathered, "tensor", j) for j in range(1, teams)]

    return pl.pallas_call(
        functools.partial(finish_kernel, parts, teams),
        out_shape=jax.ShapeDtypeStruct((steps, rows, model), BF16),
        in_specs=[SMEM, VMEM] + [VMEM] * teams,
        out_specs=VMEM,
        compiler_params=params(16),
        name="add_rows",
    )(index, layer_input_rows, *pieces)


def solution(mesh):
    placed = (
        P(None, ("groups", "fsdp"), None),
        P(),
        P("fsdp", "tensor", None),
        P("tensor", None, "fsdp"),
        P("fsdp", None),
        P("tensor", "fsdp", None),
        P("tensor", "fsdp", None),
        P("fsdp", None),
        P(("groups", "fsdp"), "tensor", None, None),
        P(("groups", "fsdp"), "tensor", None, None),
        P(("groups", "fsdp")),
    )
    return jax.shard_map(
        per_device,
        mesh=mesh,
        in_specs=placed,
        out_specs=P(None, ("groups", "fsdp"), None),
        check_vma=False,
    )
```

time: 303 us -> 79.4 us (0.26)
  local copies, waits for them, and re-layouts: 97.3 us -> 3.44 us
  blocking collectives: 80.6 us -> 0 us
  other arithmetic: 53.2 us -> 0 us
  starting transfers between devices: 6.27 us -> 25.1 us
  matrix products: 18.8 us -> 0 us
  between operations: 13.9 us -> 0.11 us
  Pallas kernels: 0 us -> 13.3 us
  waiting for transfers between devices: 31.3 us -> 37.3 us
    unnamed x21 -> x20, local copies, waits for them, and re-layouts: 47.4 us -> 3.44 us
    all_gather x3 -> x0, blocking collectives: 42.2 us -> none  [the longest x1 14.5 us: per_device(): lax.all_gather(query_up_factor, 'fsdp', axis=1, tiled=True)]
    ppermute x0 -> x18, waiting for transfers between devices: none -> 37.3 us  [swap(): return lax.ppermute(x, axis, [(i, i ^ mask) for i in range(size)])]
    psum x1 -> x0, waiting for transfers between devices: 29.8 us -> none  [per_device(): lax.psum(partial_out.astype(jnp.bfloat16), 'tensor').astype(jnp.float32)]
    unnamed x1 -> x0, blocking collectives: 26.1 us -> none
    ppermute x0 -> x18, starting transfers between devices: none -> 25.1 us  [swap(): return lax.ppermute(x, axis, [(i, i ^ mask) for i in range(size)])]
    unnamed x1 -> x0, other arithmetic: 24.5 us -> none
    dot_general x8 -> x0, matrix products: 18.8 us -> none  [the longest x1 5.02 us: per_device(): jnp.einsum('xu,gxw->ugw', qa_cols, qb_all, preferred_element_type=jnp.flo...]
  transfers between devices with their start and end apart: 4 -> 18, of which waited for: 1 -> 9; matrix products, arithmetic and copies ran while one was open for 45% -> 0% of each run, Pallas kernels for 0% -> 3%
where the time goes in v1:
time: 79.4 us; the launch traced here: 79.2 us
  waiting for transfers between devices  37.3 us (47%)
  starting transfers between devices  25.1 us (32%)
  Pallas kernels  13.3 us (17%)
  local copies, waits for them, and re-layouts  3.44 us (4%)
    ppermute x18, waiting for transfers between devices, swap(): return lax.ppermute(x, axis, [(i, i ^ mask) for i in range(size)])  37.3 us
    ppermute x18, starting transfers between devices, swap(): return lax.ppermute(x, axis, [(i, i ^ mask) for i in range(size)])  25.1 us
    pallas_call x1, Pallas kernels, per_device(): pl.pallas_call(functools.partial(project_kernel, parts, blocks), out_shap...  5.48 us
    pallas_call x1, Pallas kernels, per_device(): pl.pallas_call(functools.partial(output_kernel, parts, blocks), out_shape...  4.5 us
    unnamed x20, local copies, waits for them, and re-layouts  3.44 us
    pallas_call x1, Pallas kernels, per_device(): pl.pallas_call(functools.partial(attend_kernel, parts, rows), out_shape=j...  2.42 us
  transfers between devices with their start and end apart: 18, of which 9 were waited for; matrix products, arithmetic and copies ran while one was open for 0% of the time, Pallas kernels for 3%

profile of v1, /device:TPU:0, one launch (start us, length us, event | category | flops | bytes accessed | tf_op | source)
XLA Modules:
  0.0 79.2 jit_solution(6545618750482530199)
XLA Ops:
  0.0 5.0 %collective-permute-start.2 = (bf16[4,2,8192]{2,1,0:T(2,128)(2,1)}, bf16[4,2,8192]{2,1,0:T(2,128)(2,1)S(1)}, u32[]{:S(2)}, u32[]{:S(2)}) collective-permute-start(bf16[4,2,8192]{2,1,0:T(2,128)(2,1)} %x.1), channel_id=1, source_target_pairs={{0,12},{4,8},{8,4},{12,0},{1,13},{5,9},{9,5},{13,1},{2,14},{6,10},... | collective-permute-start | bytes 393224 | tf_op jit(solution)/shard_map/ppermute | solution.py:47
  5.7 4.0 %collective-permute-done.2.refs_3_ = bf16[4,2,8192]{2,1,0:T(2,128)(2,1)S(1)} collective-permute-done((bf16[4,2,8192]{2,1,0:T(2,128)(2,1)}, bf16[4,2,8192]{2,1,0:T(2,128)(2,1)S(1)}, u32[]{:S(2)}, u32[]{:S(2)}) %collective-permute-start.2) | collective-permute-done | bytes 131104 | tf_op jit(solution)/shard_map/ppermute | solution.py:47
  9.7 6.6 %collective-permute-done.1.refs_2_ = bf16[4,2,8192]{2,1,0:T(2,128)(2,1)S(1)} collective-permute-done((bf16[4,2,8192]{2,1,0:T(2,128)(2,1)}, bf16[4,2,8192]{2,1,0:T(2,128)(2,1)S(1)}, u32[]{:S(2)}, u32[]{:S(2)}) %collective-permute-start.1) | collective-permute-done | bytes 131104 | tf_op jit(solution)/shard_map/ppermute | solution.py:47
  17.2 0.9 %copy-done.4 = bf16[16,8192]{1,0:T(8,128)(2,1)S(1)} copy-done((bf16[16,8192]{1,0:T(8,128)(2,1)S(1)}, bf16[16,8192]{1,0:T(8,128)(2,1)}, u32[]{:S(2)}) %copy-start.4) | copy-done | bytes 262168
  19.8 5.5 %norm_project.1 = (f32[8,2560]{1,0:T(8,128)S(1)}, f32[8,2560]{1,0:T(8,128)S(1)}, f32[8,2560]{1,0:T(8,128)S(1)}, f32[8,2560]{1,0:T(8,128)S(1)}) custom-call(s32[1]{0:T(128)} %bitcast.index, bf16[4,2,8192]{2,1,0:T(2,128)(2,1)S(1)} %copy-done.2, bf16[4,2,8192]{2,1,0:T(2,128)(2,1)S(1)} %collective-permute-done.refs_1_, ...), custom_call_target="tpu_custom_call" | custom-call | tf_op jit(solution)/shard_map/norm_project/pallas_call | solution.py:268
  25.4 2.1 %collective-permute-start.9 = (bf16[16,4096]{1,0:T(8,128)(2,1)S(1)}, bf16[16,4096]{1,0:T(8,128)(2,1)S(1)}, u32[]{:S(2)}, u32[]{:S(2)}) collective-permute-start(bf16[16,4096]{1,0:T(8,128)(2,1)S(1)} %get-tuple-element.22), channel_id=1, source_target_pairs={{0,4},{4,0},{8,12},{12,8},{1,5},{5,1},{9,13},{13,9},{2,6},{6,2},{1... | collective-permute-start | bytes 393224 | tf_op jit(solution)/shard_map/ppermute | solution.py:47
  27.5 1.1 %collective-permute-start.10 = (bf16[16,4096]{1,0:T(8,128)(2,1)S(1)}, bf16[16,4096]{1,0:T(8,128)(2,1)S(1)}, u32[]{:S(2)}, u32[]{:S(2)}) collective-permute-start(bf16[16,4096]{1,0:T(8,128)(2,1)S(1)} %get-tuple-element.23), channel_id=1, source_target_pairs={{0,8},{4,12},{8,0},{12,4},{1,9},{5,13},{9,1},{13,5},{2,10},{6,14},... | collective-permute-start | bytes 393224 | tf_op jit(solution)/shard_map/ppermute | solution.py:47
  28.5 1.4 %collective-permute-start.11 = (bf16[16,4096]{1,0:T(8,128)(2,1)S(1)}, bf16[16,4096]{1,0:T(8,128)(2,1)S(1)}, u32[]{:S(2)}, u32[]{:S(2)}) collective-permute-start(bf16[16,4096]{1,0:T(8,128)(2,1)S(1)} %get-tuple-element.24), channel_id=1, source_target_pairs={{0,12},{4,8},{8,4},{12,0},{1,13},{5,9},{9,5},{13,1},{2,14},{6,10},... | collective-permute-start | bytes 393224 | tf_op jit(solution)/shard_map/ppermute | solution.py:47
  29.9 2.0 %collective-permute-start.4 = (f32[8,2560]{1,0:T(8,128)S(1)}, f32[8,2560]{1,0:T(8,128)S(1)}, u32[]{:S(2)}, u32[]{:S(2)}) collective-permute-start(f32[8,2560]{1,0:T(8,128)S(1)} %get-tuple-element.19), channel_id=1, source_target_pairs={{0,8},{4,12},{8,0},{12,4},{1,9},{5,13},{9,1},{13,5},{2,10},{6,14},... | collective-permute-start | bytes 245768 | tf_op jit(solution)/shard_map/ppermute | solution.py:47
  32.0 2.0 %collective-permute-start.5 = (f32[8,2560]{1,0:T(8,128)S(1)}, f32[8,2560]{1,0:T(8,128)S(1)}, u32[]{:S(2)}, u32[]{:S(2)}) collective-permute-start(f32[8,2560]{1,0:T(8,128)S(1)} %get-tuple-element.20), channel_id=1, source_target_pairs={{0,12},{4,8},{8,4},{12,0},{1,13},{5,9},{9,5},{13,1},{2,14},{6,10},... | collective-permute-start | bytes 245768 | tf_op jit(solution)/shard_map/ppermute | solution.py:47
  33.9 13.0 %collective-permute-done.4.refs_2_ = f32[8,2560]{1,0:T(8,128)S(1)} collective-permute-done((f32[8,2560]{1,0:T(8,128)S(1)}, f32[8,2560]{1,0:T(8,128)S(1)}, u32[]{:S(2)}, u32[]{:S(2)}) %collective-permute-start.4) | collective-permute-done | bytes 81952 | tf_op jit(solution)/shard_map/ppermute | solution.py:47
  47.0 2.4 %attend.1.refs_0_ = bf16[8,2048]{1,0:T(8,128)(2,1)S(1)} custom-call(s32[2]{0:T(128)S(1)} %copy-done.9, f32[8,2560]{1,0:T(8,128)S(1)} %get-tuple-element.17.refs_0_, f32[8,2560]{1,0:T(8,128)S(1)} %collective-permute-done.3.refs_1_, f32[8,2560]{1,0:T(8,128)S(1)} %collective-permute-done.4.refs_2_, f32[8,2560]{1,0:T(8,128)S(1)} %collective-permute-done.5.refs_3_, ...), custom_call_target="tpu_custom_call" | custom-call | tf_op jit(solution)/shard_map/attend/pallas_call | solution.py:284
  49.4 2.4 %collective-permute-start.8 = (bf16[8,2048]{1,0:T(8,128)(2,1)S(1)}, bf16[8,2048]{1,0:T(8,128)(2,1)S(1)}, u32[]{:S(2)}, u32[]{:S(2)}) collective-permute-start(bf16[8,2048]{1,0:T(8,128)(2,1)S(1)} %attend.1.refs_0_), channel_id=1, source_target_pairs={{0,12},{4,8},{8,4},{12,0},{1,13},{5,9},{9,5},{13,1},{2,14},{6,10},... | collective-permute-start | bytes 98312 | tf_op jit(solution)/shard_map/ppermute | solution.py:47
  52.4 1.5 %collective-permute-start.6 = (bf16[8,2048]{1,0:T(8,128)(2,1)S(1)}, bf16[8,2048]{1,0:T(8,128)(2,1)S(1)}, u32[]{:S(2)}, u32[]{:S(2)}) collective-permute-start(bf16[8,2048]{1,0:T(8,128)(2,1)S(1)} %attend.1.refs_0_), channel_id=1, source_target_pairs={{0,4},{4,0},{8,12},{12,8},{1,5},{5,1},{9,13},{13,9},{2,6},{6,2},{1... | collective-permute-start | bytes 98312 | tf_op jit(solution)/shard_map/ppermute | solution.py:47
  53.9 1.3 %collective-permute-done.8.refs_3_ = bf16[8,2048]{1,0:T(8,128)(2,1)S(1)} collective-permute-done((bf16[8,2048]{1,0:T(8,128)(2,1)S(1)}, bf16[8,2048]{1,0:T(8,128)(2,1)S(1)}, u32[]{:S(2)}, u32[]{:S(2)}) %collective-permute-start.8) | collective-permute-done | bytes 32800 | tf_op jit(solution)/shard_map/ppermute | solution.py:47
  55.2 1.7 %collective-permute-done.7.refs_2_ = bf16[8,2048]{1,0:T(8,128)(2,1)S(1)} collective-permute-done((bf16[8,2048]{1,0:T(8,128)(2,1)S(1)}, bf16[8,2048]{1,0:T(8,128)(2,1)S(1)}, u32[]{:S(2)}, u32[]{:S(2)}) %collective-permute-start.7) | collective-permute-done | bytes 32800 | tf_op jit(solution)/shard_map/ppermute | solution.py:47
  56.9 4.5 %project_out.1 = (bf16[8,2048]{1,0:T(8,128)(2,1)S(1)}, bf16[8,2048]{1,0:T(8,128)(2,1)S(1)}, bf16[8,2048]{1,0:T(8,128)(2,1)S(1)}, bf16[8,2048]{1,0:T(8,128)(2,1)S(1)}) custom-call(bf16[8,2048]{1,0:T(8,128)(2,1)S(1)} %attend.1.refs_0_, bf16[8,2048]{1,0:T(8,128)(2,1)S(1)} %collective-permute-done.6.refs_1_, bf16[8,2048]{1,0:T(8,128)(2,1)S(1)} %collective-permute-done.7.refs_2_, ...), custom_call_target="tpu_custom_call" | custom-call | tf_op jit(solution)/shard_map/project_out/pallas_call | solution.py:294
  62.4 1.6 %collective-permute-start.13 = (bf16[8,2048]{1,0:T(8,128)(2,1)S(1)}, bf16[8,2048]{1,0:T(8,128)(2,1)S(1)}, u32[]{:S(2)}, u32[]{:S(2)}) collective-permute-start(bf16[8,2048]{1,0:T(8,128)(2,1)S(1)} %get-tuple-element.27), channel_id=1, source_target_pairs={{0,8},{4,12},{8,0},{12,4},{1,9},{5,13},{9,1},{13,5},{2,10},{6,14},... | collective-permute-start | bytes 98312 | tf_op jit(solution)/shard_map/ppermute | solution.py:47
  63.9 1.9 %collective-permute-start.14 = (bf16[8,2048]{1,0:T(8,128)(2,1)S(1)}, bf16[8,2048]{1,0:T(8,128)(2,1)S(1)}, u32[]{:S(2)}, u32[]{:S(2)}) collective-permute-start(bf16[8,2048]{1,0:T(8,128)(2,1)S(1)} %get-tuple-element.28), channel_id=1, source_target_pairs={{0,12},{4,8},{8,4},{12,0},{1,13},{5,9},{9,5},{13,1},{2,14},{6,10},... | collective-permute-start | bytes 98312 | tf_op jit(solution)/shard_map/ppermute | solution.py:47
  65.9 1.3 %collective-permute-done.13.refs_2_ = bf16[8,2048]{1,0:T(8,128)(2,1)S(1)} collective-permute-done((bf16[8,2048]{1,0:T(8,128)(2,1)S(1)}, bf16[8,2048]{1,0:T(8,128)(2,1)S(1)}, u32[]{:S(2)}, u32[]{:S(2)}) %collective-permute-start.13) | collective-permute-done | bytes 32800 | tf_op jit(solution)/shard_map/ppermute | solution.py:47
  67.2 2.5 %collective-permute-done.14.refs_3_ = bf16[8,2048]{1,0:T(8,128)(2,1)S(1)} collective-permute-done((bf16[8,2048]{1,0:T(8,128)(2,1)S(1)}, bf16[8,2048]{1,0:T(8,128)(2,1)S(1)}, u32[]{:S(2)}, u32[]{:S(2)}) %collective-permute-start.14) | collective-permute-done | bytes 32800 | tf_op jit(solution)/shard_map/ppermute | solution.py:47
  69.7 1.6 %collective-permute-start.16 = (bf16[8,8192]{1,0:T(8,128)(2,1)S(1)}, bf16[8,8192]{1,0:T(8,128)(2,1)S(1)}, u32[]{:S(2)}, u32[]{:S(2)}) collective-permute-start(bf16[8,8192]{1,0:T(8,128)(2,1)S(1)} %gather_columns.1.refs_0_), channel_id=1, source_target_pairs={{0,2},{1,3},{2,0},{3,1},{4,6},{5,7},{6,4},{7,5},{8,10},{9,11},{10,... | collective-permute-start | bytes 393224 | tf_op jit(solution)/shard_map/ppermute | solution.py:47
  71.6 3.9 %collective-permute-done.17.refs_3_ = bf16[8,8192]{1,0:T(8,128)(2,1)S(1)} collective-permute-done((bf16[8,8192]{1,0:T(8,128)(2,1)S(1)}, bf16[8,8192]{1,0:T(8,128)(2,1)S(1)}, u32[]{:S(2)}, u32[]{:S(2)}) %collective-permute-start.17) | collective-permute-done | bytes 131104 | tf_op jit(solution)/shard_map/ppermute | solution.py:47
  75.5 2.9 %collective-permute-done.16.refs_2_ = bf16[8,8192]{1,0:T(8,128)(2,1)S(1)} collective-permute-done((bf16[8,8192]{1,0:T(8,128)(2,1)S(1)}, bf16[8,8192]{1,0:T(8,128)(2,1)S(1)}, u32[]{:S(2)}, u32[]{:S(2)}) %collective-permute-start.16) | collective-permute-done | bytes 131104 | tf_op jit(solution)/shard_map/ppermute | solution.py:47
  (38 shorter events, 6.0 us)
Async XLA Ops:
  0.0 47.0 %copy-start = (bf16[2,2,2048,128]{3,2,1,0:T(8,128)(2,1)S(1)}, bf16[2,2,2048,128]{3,2,1,0:T(8,128)(2,1)}, u32[]{:S(2)}) copy-start(bf16[2,2,2048,128]{3,2,1,0:T(8,128)(2,1)} %refs_4_.3) | copy-start | bytes 6291460
  0.0 9.7 %collective-permute-start.2 = (bf16[4,2,8192]{2,1,0:T(2,128)(2,1)}, bf16[4,2,8192]{2,1,0:T(2,128)(2,1)S(1)}, u32[]{:S(2)}, u32[]{:S(2)}) collective-permute-start(bf16[4,2,8192]{2,1,0:T(2,128)(2,1)} %x.1), channel_id=1, source_target_pairs={{0,12},{4,8},{8,4},{12,0},{1,13},{5,9},{9,5},{13,1},{2,14},{6,10},... | collective-permute-start | bytes 393224 | tf_op jit(solution)/shard_map/ppermute | solution.py:47
  5.1 11.3 %collective-permute-start.1 = (bf16[4,2,8192]{2,1,0:T(2,128)(2,1)}, bf16[4,2,8192]{2,1,0:T(2,128)(2,1)S(1)}, u32[]{:S(2)}, u32[]{:S(2)}) collective-permute-start(bf16[4,2,8192]{2,1,0:T(2,128)(2,1)} %x.1), channel_id=1, source_target_pairs={{0,8},{4,12},{8,0},{12,4},{1,9},{5,13},{9,1},{13,5},{2,10},{6,14},... | collective-permute-start | bytes 393224 | tf_op jit(solution)/shard_map/ppermute | solution.py:47
  5.1 11.3 %collective-permute-start = (bf16[4,2,8192]{2,1,0:T(2,128)(2,1)}, bf16[4,2,8192]{2,1,0:T(2,128)(2,1)S(1)}, u32[]{:S(2)}, u32[]{:S(2)}) collective-permute-start(bf16[4,2,8192]{2,1,0:T(2,128)(2,1)} %x.1), channel_id=1, source_target_pairs={{0,4},{4,0},{8,12},{12,8},{1,5},{5,1},{9,13},{13,9},{2,6},{6,2},{1... | collective-permute-start | bytes 393224 | tf_op jit(solution)/shard_map/ppermute | solution.py:47
  5.7 41.3 %copy-start.1 = (bf16[2,2,2048,128]{3,2,1,0:T(8,128)(2,1)S(1)}, bf16[2,2,2048,128]{3,2,1,0:T(8,128)(2,1)}, u32[]{:S(2)}) copy-start(bf16[2,2,2048,128]{3,2,1,0:T(8,128)(2,1)} %refs_5_.3) | copy-start | bytes 6291460
  19.8 5.6 %copy-start.5 = (bf16[16,8192]{1,0:T(8,128)(2,1)S(1)}, bf16[16,8192]{1,0:T(8,128)(2,1)}, u32[]{:S(2)}) copy-start(bf16[16,8192]{1,0:T(8,128)(2,1)} %up.1) | copy-start | bytes 786436
  19.8 5.6 %copy-start.7 = (bf16[2,16,1024]{2,1,0:T(8,128)(2,1)S(1)}, bf16[2,16,1024]{2,1,0:T(8,128)(2,1)}, u32[]{:S(2)}) copy-start(bf16[2,16,1024]{2,1,0:T(8,128)(2,1)} %down.1) | copy-start | bytes 196612
  19.8 27.2 %copy-start.9 = (s32[2]{0:T(128)S(1)}, s32[2]{0:T(128)}, u32[]{:S(2)}) copy-start(s32[2]{0:T(128)} %lengths.1) | copy-start | bytes 28
  25.2 53.1 %copy-start.3 = (bf16[4,2,8192]{2,1,0:T(2,128)(2,1)S(1)}, bf16[4,2,8192]{2,1,0:T(2,128)(2,1)}, u32[]{:S(2)}) copy-start(bf16[4,2,8192]{2,1,0:T(2,128)(2,1)} %x.1) | copy-start | bytes 393220
  25.3 6.7 %collective-permute-start.3 = (f32[8,2560]{1,0:T(8,128)S(1)}, f32[8,2560]{1,0:T(8,128)S(1)}, u32[]{:S(2)}, u32[]{:S(2)}) collective-permute-start(f32[8,2560]{1,0:T(8,128)S(1)} %get-tuple-element.18), channel_id=1, source_target_pairs={{0,4},{4,0},{8,12},{12,8},{1,5},{5,1},{9,13},{13,9},{2,6},{6,2},{1... | collective-permute-start | bytes 245768 | tf_op jit(solution)/shard_map/ppermute | solution.py:47
  25.4 27.0 %collective-permute-start.9 = (bf16[16,4096]{1,0:T(8,128)(2,1)S(1)}, bf16[16,4096]{1,0:T(8,128)(2,1)S(1)}, u32[]{:S(2)}, u32[]{:S(2)}) collective-permute-start(bf16[16,4096]{1,0:T(8,128)(2,1)S(1)} %get-tuple-element.22), channel_id=1, source_target_pairs={{0,4},{4,0},{8,12},{12,8},{1,5},{5,1},{9,13},{13,9},{2,6},{6,2},{1... | collective-permute-start | bytes 393224 | tf_op jit(solution)/shard_map/ppermute | solution.py:47
  27.5 26.4 %collective-permute-start.10 = (bf16[16,4096]{1,0:T(8,128)(2,1)S(1)}, bf16[16,4096]{1,0:T(8,128)(2,1)S(1)}, u32[]{:S(2)}, u32[]{:S(2)}) collective-permute-start(bf16[16,4096]{1,0:T(8,128)(2,1)S(1)} %get-tuple-element.23), channel_id=1, source_target_pairs={{0,8},{4,12},{8,0},{12,4},{1,9},{5,13},{9,1},{13,5},{2,10},{6,14},... | collective-permute-start | bytes 393224 | tf_op jit(solution)/shard_map/ppermute | solution.py:47
  28.5 25.3 %collective-permute-start.11 = (bf16[16,4096]{1,0:T(8,128)(2,1)S(1)}, bf16[16,4096]{1,0:T(8,128)(2,1)S(1)}, u32[]{:S(2)}, u32[]{:S(2)}) collective-permute-start(bf16[16,4096]{1,0:T(8,128)(2,1)S(1)} %get-tuple-element.24), channel_id=1, source_target_pairs={{0,12},{4,8},{8,4},{12,0},{1,13},{5,9},{9,5},{13,1},{2,14},{6,10},... | collective-permute-start | bytes 393224 | tf_op jit(solution)/shard_map/ppermute | solution.py:47
  29.9 17.0 %collective-permute-start.4 = (f32[8,2560]{1,0:T(8,128)S(1)}, f32[8,2560]{1,0:T(8,128)S(1)}, u32[]{:S(2)}, u32[]{:S(2)}) collective-permute-start(f32[8,2560]{1,0:T(8,128)S(1)} %get-tuple-element.19), channel_id=1, source_target_pairs={{0,8},{4,12},{8,0},{12,4},{1,9},{5,13},{9,1},{13,5},{2,10},{6,14},... | collective-permute-start | bytes 245768 | tf_op jit(solution)/shard_map/ppermute | solution.py:47
  32.0 15.0 %collective-permute-start.5 = (f32[8,2560]{1,0:T(8,128)S(1)}, f32[8,2560]{1,0:T(8,128)S(1)}, u32[]{:S(2)}, u32[]{:S(2)}) collective-permute-start(f32[8,2560]{1,0:T(8,128)S(1)} %get-tuple-element.20), channel_id=1, source_target_pairs={{0,12},{4,8},{8,4},{12,0},{1,13},{5,9},{9,5},{13,1},{2,14},{6,10},... | collective-permute-start | bytes 245768 | tf_op jit(solution)/shard_map/ppermute | solution.py:47
  49.4 5.8 %collective-permute-start.8 = (bf16[8,2048]{1,0:T(8,128)(2,1)S(1)}, bf16[8,2048]{1,0:T(8,128)(2,1)S(1)}, u32[]{:S(2)}, u32[]{:S(2)}) collective-permute-start(bf16[8,2048]{1,0:T(8,128)(2,1)S(1)} %attend.1.refs_0_), channel_id=1, source_target_pairs={{0,12},{4,8},{8,4},{12,0},{1,13},{5,9},{9,5},{13,1},{2,14},{6,10},... | collective-permute-start | bytes 98312 | tf_op jit(solution)/shard_map/ppermute | solution.py:47
  51.8 5.1 %collective-permute-start.7 = (bf16[8,2048]{1,0:T(8,128)(2,1)S(1)}, bf16[8,2048]{1,0:T(8,128)(2,1)S(1)}, u32[]{:S(2)}, u32[]{:S(2)}) collective-permute-start(bf16[8,2048]{1,0:T(8,128)(2,1)S(1)} %attend.1.refs_0_), channel_id=1, source_target_pairs={{0,8},{4,12},{8,0},{12,4},{1,9},{5,13},{9,1},{13,5},{2,10},{6,14},... | collective-permute-start | bytes 98312 | tf_op jit(solution)/shard_map/ppermute | solution.py:47
  52.4 4.5 %collective-permute-start.6 = (bf16[8,2048]{1,0:T(8,128)(2,1)S(1)}, bf16[8,2048]{1,0:T(8,128)(2,1)S(1)}, u32[]{:S(2)}, u32[]{:S(2)}) collective-permute-start(bf16[8,2048]{1,0:T(8,128)(2,1)S(1)} %attend.1.refs_0_), channel_id=1, source_target_pairs={{0,4},{4,0},{8,12},{12,8},{1,5},{5,1},{9,13},{13,9},{2,6},{6,2},{1... | collective-permute-start | bytes 98312 | tf_op jit(solution)/shard_map/ppermute | solution.py:47
  61.4 4.5 %collective-permute-start.12 = (bf16[8,2048]{1,0:T(8,128)(2,1)S(1)}, bf16[8,2048]{1,0:T(8,128)(2,1)S(1)}, u32[]{:S(2)}, u32[]{:S(2)}) collective-permute-start(bf16[8,2048]{1,0:T(8,128)(2,1)S(1)} %get-tuple-element.26), channel_id=1, source_target_pairs={{0,4},{4,0},{8,12},{12,8},{1,5},{5,1},{9,13},{13,9},{2,6},{6,2},{1... | collective-permute-start | bytes 98312 | tf_op jit(solution)/shard_map/ppermute | solution.py:47
  62.4 4.8 %collective-permute-start.13 = (bf16[8,2048]{1,0:T(8,128)(2,1)S(1)}, bf16[8,2048]{1,0:T(8,128)(2,1)S(1)}, u32[]{:S(2)}, u32[]{:S(2)}) collective-permute-start(bf16[8,2048]{1,0:T(8,128)(2,1)S(1)} %get-tuple-element.27), channel_id=1, source_target_pairs={{0,8},{4,12},{8,0},{12,4},{1,9},{5,13},{9,1},{13,5},{2,10},{6,14},... | collective-permute-start | bytes 98312 | tf_op jit(solution)/shard_map/ppermute | solution.py:47
  63.9 5.7 %collective-permute-start.14 = (bf16[8,2048]{1,0:T(8,128)(2,1)S(1)}, bf16[8,2048]{1,0:T(8,128)(2,1)S(1)}, u32[]{:S(2)}, u32[]{:S(2)}) collective-permute-start(bf16[8,2048]{1,0:T(8,128)(2,1)S(1)} %get-tuple-element.28), channel_id=1, source_target_pairs={{0,12},{4,8},{8,4},{12,0},{1,13},{5,9},{9,5},{13,1},{2,14},{6,10},... | collective-permute-start | bytes 98312 | tf_op jit(solution)/shard_map/ppermute | solution.py:47
  69.7 5.8 %collective-permute-start.17 = (bf16[8,8192]{1,0:T(8,128)(2,1)S(1)}, bf16[8,8192]{1,0:T(8,128)(2,1)S(1)}, u32[]{:S(2)}, u32[]{:S(2)}) collective-permute-start(bf16[8,8192]{1,0:T(8,128)(2,1)S(1)} %gather_columns.1.refs_0_), channel_id=1, source_target_pairs={{0,3},{1,2},{2,1},{3,0},{4,7},{5,6},{6,5},{7,4},{8,11},{9,10},{10,... | collective-permute-start | bytes 393224 | tf_op jit(solution)/shard_map/ppermute | solution.py:47
  69.7 8.6 %collective-permute-start.16 = (bf16[8,8192]{1,0:T(8,128)(2,1)S(1)}, bf16[8,8192]{1,0:T(8,128)(2,1)S(1)}, u32[]{:S(2)}, u32[]{:S(2)}) collective-permute-start(bf16[8,8192]{1,0:T(8,128)(2,1)S(1)} %gather_columns.1.refs_0_), channel_id=1, source_target_pairs={{0,2},{1,3},{2,0},{3,1},{4,6},{5,7},{6,4},{7,5},{8,10},{9,11},{10,... | collective-permute-start | bytes 393224 | tf_op jit(solution)/shard_map/ppermute | solution.py:47
  71.3 7.0 %collective-permute-start.15 = (bf16[8,8192]{1,0:T(8,128)(2,1)S(1)}, bf16[8,8192]{1,0:T(8,128)(2,1)S(1)}, u32[]{:S(2)}, u32[]{:S(2)}) collective-permute-start(bf16[8,8192]{1,0:T(8,128)(2,1)S(1)} %gather_columns.1.refs_0_), channel_id=1, source_target_pairs={{0,1},{1,0},{2,3},{3,2},{4,5},{5,4},{6,7},{7,6},{8,9},{9,8},{10,11... | collective-permute-start | bytes 393224 | tf_op jit(solution)/shard_map/ppermute | solution.py:47
  (4 other events, 3.4 us)
